TPU v7x, 32 devices: a whole 2x2x4 slice. The times are simulated.
32 devices in a mesh: sub: 8 (over z, x), col: 4 (over y, core).
Axes of the slice: x: 2, y: 2, z: 4, core: 2. Of those that a mesh axis runs over, the one named last changes fastest.
Arguments:
- leaf_basis: bfloat16 [8, 4, 2048, 512], P('sub', 'col'), as said below
- transfers: bfloat16 [8, 4, 3, 512, 512], P('sub', 'col'), as said below
- couplings: bfloat16 [8, 4, 6, 512, 512], P('sub', 'col'), may hold values from -0.25 to 0.25
- partners: int32 [8, 4, 6], P('sub', 'col'), may hold values from 0 to 3
Outputs:
- q_leaf: bfloat16 [8, 4, 2048, 512], P('sub', 'col')
- root_triangle: bfloat16 [8, 4, 512, 512], P('sub', 'col')
- coupled: bfloat16 [8, 4, 6, 512, 512], P('sub', 'col')
Inputs may be any that keep to these rules, and one draw needn't show every extreme that they name: partners[s,c,k] names the leaf cluster (s, partners[s,c,k]) as column cluster; entries may repeat. Every transfer matrix is a positive diagonal plus a dense part; transfers[s,c,l] is equal for all s with the same s >> l. `leaf_basis`: every leaf basis has full column rank.
All inputs are finite; a program needn't handle non-finite values.
Results may differ from a plain program's by a relative error of at most 0.0063.
Values may be sent and summed in bfloat16 or wider, within the bound.
A program may use at most 128 MiB of HBM per device.

v0:
```python
import jax
import jax.numpy as jnp
from jax import lax
from jax.sharding import PartitionSpec as P

highest = lax.Precision.HIGHEST


def shifted(value, axis, steps):
    count = lax.axis_size(axis)
    pairs = [(source, (source + steps) % count) for source in range(count)]
    return lax.ppermute(value, axis, pairs)


def from_partner(block, axis, stride):
    count = lax.axis_size(axis)
    route = []
    for low in range(count):
        high = low | 1 << stride
        if high != low and high < count:
            route += [(low, high), (high, low)]
    return lax.ppermute(block, axis, route)


def blocked_cholesky(matrix):
    order = matrix.shape[0]
    width = 128
    columns = []
    trailing = matrix
    for start in range(0, order, width):
        head = jnp.linalg.cholesky(trailing[:width, :width])
        lower_part = trailing[width:, :width]
        if lower_part.shape[0] > 0:
            panel = lax.linalg.triangular_solve(
                head, lower_part, left_side=False, lower=True, transpose_a=True
            )
            trailing = trailing[width:, width:] - jnp.dot(panel, panel.T, precision=highest)
            column_block = jnp.concatenate(
                [jnp.zeros((start, width), jnp.float32), head, panel], axis=0
            )
        else:
            column_block = jnp.concatenate([jnp.zeros((start, width), jnp.float32), head], axis=0)
        columns.append(column_block)
    return jnp.concatenate(columns, axis=1)


def select_shifted(rounded, slot_partners):
    count = lax.axis_size("col")
    own_index = lax.axis_index("col")
    chosen = jnp.where(
        (slot_partners == own_index)[:, None, None],
        rounded[None],
        jnp.zeros((slot_partners.shape[0],) + rounded.shape, jnp.bfloat16),
    )
    for distance in range(1, count):
        arrived = shifted(rounded, "col", distance)
        source = (own_index - distance + count) % count
        chosen = jnp.where((slot_partners == source)[:, None, None], arrived[None], chosen)
    return chosen


def project(rounded, blocks, slot_partners):
    left_product = jnp.einsum(
        "ab,kbd->kad", rounded, blocks, preferred_element_type=jnp.float32
    ).astype(jnp.bfloat16)
    chosen = select_shifted(rounded, slot_partners)
    return jnp.einsum(
        "kab,kdb->kad", left_product, chosen, preferred_element_type=jnp.float32
    ).astype(jnp.bfloat16)


def merge_levels(triangle, level_transfers):
    current = triangle
    contract = (((0,), (0,)), ((), ()))
    for level_index in range(level_transfers.shape[0]):
        moved = jnp.dot(
            current, level_transfers[level_index].astype(jnp.float32), precision=highest
        )
        own_gram = lax.dot_general(moved, moved, contract, precision=highest)
        partner_block = from_partner(moved, "sub", level_index)
        other_gram = lax.dot_general(partner_block, partner_block, contract, precision=highest)
        current = blocked_cholesky(own_gram + other_gram).T
    return current


def shards(leaf_basis, transfers, couplings, partners):
    own_basis = leaf_basis[0, 0]
    gram_leaf = lax.dot_general(
        own_basis, own_basis, (((0,), (0,)), ((), ())), preferred_element_type=jnp.float32
    )
    lower_leaf = blocked_cholesky(gram_leaf)
    q_transposed = lax.linalg.triangular_solve(
        lower_leaf, own_basis.T.astype(jnp.float32), left_side=True, lower=True
    )
    q_leaf = q_transposed.T.astype(jnp.bfloat16)
    triangle = lower_leaf.T
    rounded = triangle.astype(jnp.bfloat16)
    current = merge_levels(triangle, transfers[0, 0])
    coupled = project(rounded, couplings[0, 0], partners[0, 0])
    root_triangle = current.astype(jnp.bfloat16)
    return (q_leaf[None, None], root_triangle[None, None], coupled[None, None])


def solution(mesh):
    in_specs = (
        P("sub", "col", None, None),
        P("sub", "col", None, None, None),
        P("sub", "col", None, None, None),
        P("sub", "col", None),
    )
    out_specs = (
        P("sub", "col", None, None),
        P("sub", "col", None, None),
        P("sub", "col", None, None, None),
    )
    return jax.shard_map(shards, mesh=mesh, in_specs=in_specs, out_specs=out_specs, check_vma=False)
```

profile of v0, /device:TPU:31, one launch (start us, length us, event | category | flops | bytes accessed | tf_op | source)
XLA Modules:
  0.0 672.7 jit_solution(17705758104177757327)
XLA Ops:
  0.6 3.6 fusion.29
  5.5 2.1 copy.84
  8.5 11.7 %cholesky.254 = f32[128,128]{1,0:T(8,128)S(1)} custom-call(f32[128,128]{1,0:T(8,128)S(1)} %fusion.144), custom_call_target="Cholesky" | custom-call | tf_op jit(solution)/shard_map/jit(cholesky)/cholesky | solution.py:31
  22.2 9.8 %custom-call.24 = f32[1,128,128]{1,2,0:T(8,128)S(1)} custom-call(f32[1,128,128]{2,1,0:T(8,128)S(1)} %get-tuple-element.42), custom_call_target="InvertDiagBlocksLowerTriangular" | custom-call | tf_op jit(solution)/shard_map/triangular_solve/custom-call.0 | solution.py:34
  36.8 11.7 %cholesky.265 = f32[128,128]{1,0:T(8,128)S(1)} custom-call(f32[128,128]{1,0:T(8,128)S(1)} %fusion.142), custom_call_target="Cholesky" | custom-call | tf_op jit(solution)/shard_map/jit(cholesky)/cholesky | solution.py:31
  50.4 10.0 %custom-call.25 = f32[1,128,128]{1,2,0:T(8,128)S(1)} custom-call(f32[1,128,128]{2,1,0:T(8,128)S(1)} %get-tuple-element.40), custom_call_target="InvertDiagBlocksLowerTriangular" | custom-call | tf_op jit(solution)/shard_map/triangular_solve/custom-call.2 | solution.py:34
  66.8 12.5 %cholesky.276 = f32[128,128]{1,0:T(8,128)S(1)} custom-call(f32[128,128]{1,0:T(8,128)} %fusion.140), custom_call_target="Cholesky" | custom-call | tf_op jit(solution)/shard_map/jit(cholesky)/cholesky | solution.py:31
  81.4 11.3 %custom-call.26 = f32[1,128,128]{1,2,0:T(8,128)} custom-call(f32[1,128,128]{2,1,0:T(8,128)} %get-tuple-element.38), custom_call_target="InvertDiagBlocksLowerTriangular" | custom-call | tf_op jit(solution)/shard_map/triangular_solve/custom-call.3 | solution.py:34
  98.6 25.1 %cholesky.287 = f32[128,128]{1,0:T(8,128)} custom-call(f32[128,128]{1,0:T(8,128)} %fusion.138), custom_call_target="Cholesky" | custom-call | tf_op jit(solution)/shard_map/jit(cholesky)/cholesky | solution.py:31
  130.6 3.2 fusion.93
  135.2 4.1 bitcast_convert_fusion
  139.3 13.6 %while.1 = (s32[]{:T(128)}, f32[512,512]{1,0:T(8,128)}, s32[4,2]{0,1:T(2,128)S(1)}, f32[4,128,128]{2,1,0:T(8,128)}, s32[]{:T(128)}) while((s32[]{:T(128)}, f32[512,512]{1,0:T(8,128)}, s32[4,2]{0,1:T(2,128)S(1)}, f32[4,128,128]{2,1,0:T(8,128)}, s32[]{:T(128)}) %tuple.48), condition=%wide.while_cond, body=%wide.while_body.sunk | while | flops 2 | bytes 132205 | solution.py:92
  139.9 2.8 bitcast_dynamic-update-slice_fusion.2
  143.3 2.8 bitcast_dynamic-update-slice_fusion.2
  146.7 2.8 bitcast_dynamic-update-slice_fusion.2
  150.2 2.8 bitcast_dynamic-update-slice_fusion.2
  152.9 40.7 %custom-call.14 = f32[4,128,128]{1,2,0:T(8,128)} custom-call(f32[4,128,128]{2,1,0:T(8,128)} %get-tuple-element.14), custom_call_target="InvertDiagBlocksLowerTriangular" | custom-call | tf_op jit(solution)/shard_map/triangular_solve | solution.py:92
  193.7 2.5 fusion.163
  196.2 3.2 convolution_subtract_fusion.1
  201.4 4.5 convolution_subtract_fusion
  207.8 7.7 %fusion.19 = f32[128,2048]{0,1:T(8,128)} fusion(f32[128,2048]{1,0:T(8,128)S(1)} %get-tuple-element.51, f32[128,2048]{1,0:T(8,128)S(1)} %get-tuple-element.53, f32[128,2048]{1,0:T(8,128)S(1)} %get-tuple-element.55, f32[512,2048]{0,1:T(8,128)S(1)} %copy-done.1, f32[512,512]{1,0:T(8,128)} %get-tuple-element.110), kind=kOutput, calls=%fused_computation.22 | convolution fusion | flops 1209794560 | bytes 5439488 | tf_op jit(solution)/shard_map/triangular_solve | solution.py:92
  215.5 3.4 fusion.167
  218.9 3.4 convolution_add_fusion.2
  227.0 13.2 %cholesky.298 = f32[128,128]{1,0:T(8,128)} custom-call(f32[128,128]{1,0:T(8,128)} %fusion.137), custom_call_target="Cholesky" | custom-call | tf_op jit(solution)/shard_map/jit(cholesky)/cholesky | solution.py:31
  241.8 2.1 select_bitcast_fusion.8
  243.9 11.3 %custom-call.27 = f32[1,128,128]{1,2,0:T(8,128)} custom-call(f32[1,128,128]{2,1,0:T(8,128)} %get-tuple-element.36), custom_call_target="InvertDiagBlocksLowerTriangular" | custom-call | tf_op jit(solution)/shard_map/triangular_solve/custom-call.0 | solution.py:34
  263.7 13.2 %cholesky.309 = f32[128,128]{1,0:T(8,128)} custom-call(f32[128,128]{1,0:T(8,128)} %fusion.135), custom_call_target="Cholesky" | custom-call | tf_op jit(solution)/shard_map/jit(cholesky)/cholesky | solution.py:31
  278.4 2.1 select_bitcast_fusion.7
  280.5 11.3 %custom-call.28 = f32[1,128,128]{1,2,0:T(8,128)} custom-call(f32[1,128,128]{2,1,0:T(8,128)} %get-tuple-element.34), custom_call_target="InvertDiagBlocksLowerTriangular" | custom-call | tf_op jit(solution)/shard_map/triangular_solve/custom-call.2 | solution.py:34
  299.5 13.2 %cholesky.320 = f32[128,128]{1,0:T(8,128)} custom-call(f32[128,128]{1,0:T(8,128)} %fusion.133), custom_call_target="Cholesky" | custom-call | tf_op jit(solution)/shard_map/jit(cholesky)/cholesky | solution.py:31
  314.2 2.1 select_bitcast_fusion.6
  316.3 11.5 %custom-call.29 = f32[1,128,128]{1,2,0:T(8,128)} custom-call(f32[1,128,128]{2,1,0:T(8,128)} %get-tuple-element.32), custom_call_target="InvertDiagBlocksLowerTriangular" | custom-call | tf_op jit(solution)/shard_map/triangular_solve/custom-call.3 | solution.py:34
  334.3 13.2 %cholesky.331 = f32[128,128]{1,0:T(8,128)} custom-call(f32[128,128]{1,0:T(8,128)} %fusion.131), custom_call_target="Cholesky" | custom-call | tf_op jit(solution)/shard_map/jit(cholesky)/cholesky | solution.py:31
  350.6 3.4 fusion.48
  354.2 2.7 convolution_convert_fusion
  356.9 2.1 copy.54
  358.9 3.1 maximum_bitcast_fusion
  362.0 4.3 copy.55
  366.9 2.0 copy.53
  368.9 2.1 copy.52
  373.0 3.4 fusion.168
  378.1 3.5 convolution_add_fusion.1
  386.3 13.2 %cholesky.342 = f32[128,128]{1,0:T(8,128)} custom-call(f32[128,128]{1,0:T(8,128)} %fusion.130), custom_call_target="Cholesky" | custom-call | tf_op jit(solution)/shard_map/jit(cholesky)/cholesky | solution.py:31
  401.0 2.1 select_bitcast_fusion.5
  403.2 11.3 %custom-call.30 = f32[1,128,128]{1,2,0:T(8,128)} custom-call(f32[1,128,128]{2,1,0:T(8,128)} %get-tuple-element.30), custom_call_target="InvertDiagBlocksLowerTriangular" | custom-call | tf_op jit(solution)/shard_map/triangular_solve/custom-call.0 | solution.py:34
  422.8 13.3 %cholesky.353 = f32[128,128]{1,0:T(8,128)} custom-call(f32[128,128]{1,0:T(8,128)} %fusion.128), custom_call_target="Cholesky" | custom-call | tf_op jit(solution)/shard_map/jit(cholesky)/cholesky | solution.py:31
  437.6 2.1 select_bitcast_fusion.4
  439.8 11.3 %custom-call.31 = f32[1,128,128]{1,2,0:T(8,128)} custom-call(f32[1,128,128]{2,1,0:T(8,128)} %get-tuple-element.28), custom_call_target="InvertDiagBlocksLowerTriangular" | custom-call | tf_op jit(solution)/shard_map/triangular_solve/custom-call.2 | solution.py:34
  458.7 13.2 %cholesky.364 = f32[128,128]{1,0:T(8,128)} custom-call(f32[128,128]{1,0:T(8,128)} %fusion.126), custom_call_target="Cholesky" | custom-call | tf_op jit(solution)/shard_map/jit(cholesky)/cholesky | solution.py:31
  473.4 2.0 select_bitcast_fusion.3
  475.4 11.5 %custom-call.32 = f32[1,128,128]{1,2,0:T(8,128)} custom-call(f32[1,128,128]{2,1,0:T(8,128)} %get-tuple-element.26), custom_call_target="InvertDiagBlocksLowerTriangular" | custom-call | tf_op jit(solution)/shard_map/triangular_solve/custom-call.3 | solution.py:34
  493.5 13.2 %cholesky.375 = f32[128,128]{1,0:T(8,128)} custom-call(f32[128,128]{1,0:T(8,128)} %fusion.124), custom_call_target="Cholesky" | custom-call | tf_op jit(solution)/shard_map/jit(cholesky)/cholesky | solution.py:31
  509.7 3.4 fusion.54
  513.2 6.9 %convert_bitcast_fusion = bf16[1,1,6,512,512]{4,3,2,1,0:T(8,128)(2,1)} fusion(pred[6]{0:T(512)(128)(4,1)S(1)} %get-tuple-element.48, pred[6]{0:T(512)(128)(4,1)S(1)} %copy-done.29, pred[6]{0:T(512)(128)(4,1)S(1)} %get-tuple-element.47, pred[6]{0:T(512)(128)(4,1)S(1)} %get-tuple-element.46, bf16[1,1,6,512,512]{4,3,2,1,0:T(8,128)(2,1)S(1)} %copy-done, ...), kind=kOutput, calls=%fused_computation.12 | convolution fusion | flops 3235905536 | bytes 9240600 | tf_op jit(solution)/shard_map/kab,kdb->kad/dot_general | solution.py:67
  520.1 3.4 fusion.169
  523.5 38.2 %collective-permute-done.2 = f32[512,512]{1,0:T(8,128)} collective-permute-done((f32[512,512]{1,0:T(8,128)}, f32[512,512]{1,0:T(8,128)}, u32[]{:S(2)}, u32[]{:S(2)}) %collective-permute-start.2) | collective-permute-done | bytes 1048608 | tf_op jit(solution)/shard_map/ppermute | solution.py:22
  561.7 4.0 convolution_add_fusion
  567.7 11.7 %cholesky.386 = f32[128,128]{1,0:T(8,128)S(1)} custom-call(f32[128,128]{1,0:T(8,128)S(1)} %fusion.123), custom_call_target="Cholesky" | custom-call | tf_op jit(solution)/shard_map/jit(cholesky)/cholesky | solution.py:31
  580.9 10.4 %custom-call.33 = f32[1,128,128]{1,2,0:T(8,128)} custom-call(f32[1,128,128]{2,1,0:T(8,128)S(1)} %select_bitcast_fusion.2), custom_call_target="InvertDiagBlocksLowerTriangular" | custom-call | tf_op jit(solution)/shard_map/triangular_solve/custom-call.0 | solution.py:34
  596.3 11.7 %cholesky.397 = f32[128,128]{1,0:T(8,128)S(1)} custom-call(f32[128,128]{1,0:T(8,128)S(1)} %fusion.121), custom_call_target="Cholesky" | custom-call | tf_op jit(solution)/shard_map/jit(cholesky)/cholesky | solution.py:31
  609.3 10.6 %custom-call.34 = f32[1,128,128]{1,2,0:T(8,128)} custom-call(f32[1,128,128]{2,1,0:T(8,128)S(1)} %select_bitcast_fusion.1), custom_call_target="InvertDiagBlocksLowerTriangular" | custom-call | tf_op jit(solution)/shard_map/triangular_solve/custom-call.2 | solution.py:34
  624.9 11.7 %cholesky.408 = f32[128,128]{1,0:T(8,128)S(1)} custom-call(f32[128,128]{1,0:T(8,128)S(1)} %fusion.119), custom_call_target="Cholesky" | custom-call | tf_op jit(solution)/shard_map/jit(cholesky)/cholesky | solution.py:31
  640.5 10.6 %custom-call.35 = f32[1,128,128]{1,2,0:T(8,128)S(1)} custom-call(f32[1,128,128]{2,1,0:T(8,128)} %select_bitcast_fusion), custom_call_target="InvertDiagBlocksLowerTriangular" | custom-call | tf_op jit(solution)/shard_map/triangular_solve/custom-call.3 | solution.py:34
  654.1 12.5 %cholesky.419 = f32[128,128]{1,0:T(8,128)S(1)} custom-call(f32[128,128]{1,0:T(8,128)} %fusion.117), custom_call_target="Cholesky" | custom-call | tf_op jit(solution)/shard_map/jit(cholesky)/cholesky | solution.py:31
  (206 shorter events, 141.0 us)
Async XLA Ops:
  0.6 512.5 %copy-start = (bf16[1,1,6,512,512]{4,3,2,1,0:T(8,128)(2,1)S(1)}, bf16[1,1,6,512,512]{4,3,2,1,0:T(8,128)(2,1)}, u32[]{:S(2)}) copy-start(bf16[1,1,6,512,512]{4,3,2,1,0:T(8,128)(2,1)} %param.13) | copy-start | bytes 9437188
  4.3 1.2 copy-start.19
  35.0 0.8 copy-start.6
  63.1 0.7 copy-start.16
  126.7 7.3 %copy-start.25 = (f32[128,128]{1,0:T(8,128)}, f32[128,128]{1,0:T(8,128)S(1)}, u32[]{:S(2)}) copy-start(f32[128,128]{1,0:T(8,128)S(1)} %select_select_fusion.11) | copy-start | bytes 196612
  126.8 7.3 %copy-start.14 = (f32[256,128]{1,0:T(8,128)}, f32[256,128]{1,0:T(8,128)S(1)}, u32[]{:S(2)}) copy-start(f32[256,128]{1,0:T(8,128)S(1)} %broadcast.118) | copy-start | bytes 393220
  126.8 7.3 %copy-start.26 = (f32[128,128]{1,0:T(8,128)}, f32[128,128]{1,0:T(8,128)S(1)}, u32[]{:S(2)}) copy-start(f32[128,128]{1,0:T(8,128)S(1)} %cholesky.255) | copy-start | bytes 196612
  128.6 5.5 copy-start.22
  128.6 5.5 copy-start.23
  128.6 5.5 copy-start.24
  128.6 238.3 %collective-permute-start.5 = (bf16[512,512]{0,1:T(8,128)(2,1)}, bf16[512,512]{0,1:T(8,128)(2,1)}, u32[]{:S(2)}, u32[]{:S(2)}) collective-permute-start(bf16[512,512]{0,1:T(8,128)(2,1)} %convert_bitcast_fusion.1), channel_id=1, source_target_pairs={{0,1},{1,2},{2,3},{3,0},{4,5},{5,6},{6,7},{7,4},{8,9},{9,10},{10,1... | collective-permute-start | bytes 1572872 | tf_op jit(solution)/shard_map/ppermute | solution.py:12
  129.4 239.5 %collective-permute-start.4 = (bf16[512,512]{0,1:T(8,128)(2,1)}, bf16[512,512]{0,1:T(8,128)(2,1)}, u32[]{:S(2)}, u32[]{:S(2)}) collective-permute-start(bf16[512,512]{0,1:T(8,128)(2,1)} %convert_bitcast_fusion.1), channel_id=1, source_target_pairs={{0,2},{1,3},{2,0},{3,1},{4,6},{5,7},{6,4},{7,5},{8,10},{9,11},{10,... | collective-permute-start | bytes 1572872 | tf_op jit(solution)/shard_map/ppermute | solution.py:12
  130.6 240.3 %collective-permute-start.3 = (bf16[512,512]{0,1:T(8,128)(2,1)}, bf16[512,512]{0,1:T(8,128)(2,1)}, u32[]{:S(2)}, u32[]{:S(2)}) collective-permute-start(bf16[512,512]{0,1:T(8,128)(2,1)} %convert_bitcast_fusion.1), channel_id=1, source_target_pairs={{0,3},{1,0},{2,1},{3,2},{4,7},{5,4},{6,5},{7,6},{8,11},{9,8},{10,9... | collective-permute-start | bytes 1572872 | tf_op jit(solution)/shard_map/ppermute | solution.py:12
  133.8 85.1 %collective-permute-start = (f32[512,512]{1,0:T(8,128)}, f32[512,512]{1,0:T(8,128)}, u32[]{:S(2)}, u32[]{:S(2)}) collective-permute-start(f32[512,512]{1,0:T(8,128)} %fusion.93), channel_id=1, source_target_pairs={{0,4},{4,0},{8,12},{12,8},{16,20},{20,16},{24,28},{28,24},{1,5},{5... | collective-permute-start | bytes 3145736 | tf_op jit(solution)/shard_map/ppermute | solution.py:22
  193.7 5.8 copy-start.27
  196.2 5.2 copy-start.1
  222.4 1.0 copy-start.3
  256.6 0.7 copy-start.10
  259.0 0.8 copy-start.7
  293.1 0.6 copy-start.12
  295.1 0.7 copy-start.17
  328.9 0.6 copy-start.20
  349.0 5.2 copy-start.2
  354.0 24.1 %collective-permute-start.1 = (f32[512,512]{1,0:T(8,128)}, f32[512,512]{1,0:T(8,128)}, u32[]{:S(2)}, u32[]{:S(2)}) collective-permute-start(f32[512,512]{1,0:T(8,128)} %fusion.48), channel_id=1, source_target_pairs={{0,8},{8,0},{4,12},{12,4},{16,24},{24,16},{20,28},{28,20},{1,9},{9... | collective-permute-start | bytes 3145736 | tf_op jit(solution)/shard_map/ppermute | solution.py:22
  362.0 4.3 copy-start.28
  381.6 1.0 copy-start.4
  415.9 0.7 copy-start.11
  418.3 0.8 copy-start.8
  452.4 0.6 copy-start.13
  454.4 0.7 copy-start.18
  488.0 0.6 copy-start.21
  508.2 5.0 copy-start.29
  513.1 48.6 %collective-permute-start.2 = (f32[512,512]{1,0:T(8,128)}, f32[512,512]{1,0:T(8,128)}, u32[]{:S(2)}, u32[]{:S(2)}) collective-permute-start(f32[512,512]{1,0:T(8,128)} %fusion.54), channel_id=1, source_target_pairs={{0,16},{16,0},{4,20},{20,4},{8,24},{24,8},{12,28},{28,12},{1,17},{... | collective-permute-start | bytes 3145736 | tf_op jit(solution)/shard_map/ppermute | solution.py:22
  565.7 1.0 copy-start.5
  594.5 0.8 copy-start.9
  623.2 0.7 copy-start.15
where the time goes:
time: 683 us; the launch traced here: 673 us
  other arithmetic  464 us (68%)
  matrix products  101 us (15%)
  local copies, waits for them, and re-layouts  64.3 us (9%)
  waiting for transfers between devices  39.9 us (6%)
    another operation x48, other arithmetic, blocked_cholesky(): head = jnp.linalg.cholesky(trailing[:width, :width])  233 us
    another operation x24, other arithmetic, blocked_cholesky(): lax.linalg.triangular_solve(head, lower_part, left_side=False, lower=True...  150 us
    another operation x3, other arithmetic, shards(): lax.linalg.triangular_solve(lower_leaf, own_basis.T.astype(jnp.float32),...  41.8 us
    ppermute x3, waiting for transfers between devices, from_partner(): return lax.ppermute(block, axis, route)  39.9 us
    another operation x7, matrix products, shards(): lax.linalg.triangular_solve(lower_leaf, own_basis.T.astype(jnp.float32),...  24.5 us
    unnamed x64, local copies, waits for them, and re-layouts  21.6 us
    div x16, other arithmetic, blocked_cholesky(): head = jnp.linalg.cholesky(trailing[:width, :width])  19.9 us
    dot_general x12, matrix products, blocked_cholesky(): jnp.dot(panel, panel.T, precision=highest)  18.5 us
  transfers between devices with their start and end apart: 6, of which 2 were waited for; matrix products, arithmetic and copies ran while one was open for 37% of the time, Pallas kernels for 0%

commit v1 on v0

v1 whole, which is shorter than its diff:
```python
import functools

import jax
import jax.numpy as jnp
from jax import lax
from jax.experimental import pallas as pl
from jax.experimental.pallas import tpu as pltpu
from jax.sharding import PartitionSpec as P

highest = lax.Precision.HIGHEST
F32 = jnp.float32
BF16 = jnp.bfloat16
LANES = 128
BLOCK = 64
ROWS = 8
CONTRACT_FIRST = (((0,), (0,)), ((), ()))
CONTRACT_LAST = (((1,), (1,)), ((), ()))


def dot_f32(a, b, dims=(((1,), (0,)), ((), ()))):
    return lax.dot_general(a, b, dims, precision=highest, preferred_element_type=F32)


def dot_bf16(a, b, dims=(((1,), (0,)), ((), ()))):
    return lax.dot_general(a, b, dims, preferred_element_type=F32)


def upper_tiles(order):
    count = order // LANES
    return [(i, j) for i in range(count) for j in range(i, count)]


def eliminate(block, offset):
    finished = []
    row_index = lax.broadcasted_iota(jnp.int32, (ROWS, LANES), 0)
    current = block
    for panel in range(BLOCK // ROWS):
        first = offset + panel * ROWS
        top = current[:ROWS]
        rest = current[ROWS:]
        below = rest.shape[0] > 0
        top_columns = [
            jnp.broadcast_to(top[:, first + j : first + j + 1], top.shape) for j in range(ROWS)
        ]
        if below:
            rest_columns = [
                jnp.broadcast_to(rest[:, first + j : first + j + 1], rest.shape)
                for j in range(ROWS)
            ]
        pivots = top_columns[0]
        for j in range(ROWS):
            inverse = 1.0 / top_columns[j][j : j + 1]
            factor = jnp.where(row_index > j, top_columns[j] * inverse, 0.0)
            if j > 0:
                pivots = jnp.where(row_index == j, top_columns[j], pivots)
            pivot_row = top[j : j + 1]
            if below:
                rest_factor = rest_columns[j] * inverse
                rest = rest - rest_factor * pivot_row
            for k in range(j + 1, ROWS):
                value = top_columns[k][j : j + 1]
                top_columns[k] = top_columns[k] - factor * value
                if below:
                    rest_columns[k] = rest_columns[k] - rest_factor * value
            top = top - factor * pivot_row
        finished.append(top * lax.rsqrt(pivots))
        current = rest
    return jnp.concatenate(finished, axis=0)


def factor(work, order, width, emit):
    extra = width > order
    lane = lax.broadcasted_iota(jnp.int32, (BLOCK, LANES), 1)
    row = lax.broadcasted_iota(jnp.int32, (BLOCK, LANES), 0)
    for start in range(0, order, BLOCK):
        base = start // LANES * LANES
        offset = start - base
        other = BLOCK - offset
        head = work[start : start + BLOCK, base : base + LANES]
        own_half = (lane >= offset) & (lane < offset + BLOCK)
        unit = jnp.where(lane == row + other, 1.0, 0.0).astype(F32)
        solved = eliminate(jnp.where(own_half, head, unit), offset)
        inverse = solved[:, other : other + BLOCK]
        end = order + base + LANES if extra else order
        panel = dot_f32(inverse, work[start : start + BLOCK, base:end])
        emit(start, base, panel)
        for low in range(base + offset * 2, order, LANES):
            shift = low - base
            work[low : low + LANES, low:end] -= dot_f32(
                panel[:, shift : shift + LANES], panel[:, shift:], CONTRACT_FIRST
            )


def gram_kernel(basis_ref, transfers_ref, gram_ref, tiles_ref):
    order = gram_ref.shape[0]
    gram_ref[...] = dot_bf16(basis_ref[...], basis_ref[...], CONTRACT_FIRST)
    moved = transfers_ref[0].astype(F32)
    for level in range(1, transfers_ref.shape[0]):
        moved = dot_f32(moved, transfers_ref[level].astype(F32))
    applied = dot_f32(gram_ref[...], moved)
    for index, (i, j) in enumerate(upper_tiles(order)):
        tiles_ref[index * LANES : (index + 1) * LANES, :] = dot_f32(
            moved[:, i * LANES : (i + 1) * LANES],
            applied[:, j * LANES : (j + 1) * LANES],
            CONTRACT_FIRST,
        )


def upper_mask(panel, start, base):
    shape = panel.shape
    lane = lax.broadcasted_iota(jnp.int32, shape, 1) + base
    row = lax.broadcasted_iota(jnp.int32, shape, 0) + start
    return jnp.where(lane >= row, panel, 0.0)


def leaf_kernel(gram_ref, rounded_ref, high_ref, low_ref, work):
    order = gram_ref.shape[0]
    work[:, :order] = gram_ref[...]
    row = lax.broadcasted_iota(jnp.int32, (order, order), 0)
    lane = lax.broadcasted_iota(jnp.int32, (order, order), 1)
    work[:, order:] = jnp.where(row == lane, 1.0, 0.0).astype(F32)
    rounded_ref[...] = jnp.zeros(rounded_ref.shape, BF16)
    high_ref[...] = jnp.zeros(high_ref.shape, BF16)
    low_ref[...] = jnp.zeros(low_ref.shape, BF16)

    def emit(start, base, panel):
        head = upper_mask(panel[:, : order - base], start, base)
        rounded_ref[start : start + BLOCK, base:] = head.astype(BF16)
        inverse = panel[:, order - base :]
        high = inverse.astype(BF16)
        high_ref[start : start + BLOCK, : base + LANES] = high
        low_ref[start : start + BLOCK, : base + LANES] = (inverse - high.astype(F32)).astype(BF16)

    factor(work, order, 2 * order, emit)


def root_kernel(tiles_ref, root_ref, work):
    order = root_ref.shape[0]
    for index, (i, j) in enumerate(upper_tiles(order)):
        work[i * LANES : (i + 1) * LANES, j * LANES : (j + 1) * LANES] = tiles_ref[
            index * LANES : (index + 1) * LANES, :
        ]
    root_ref[...] = jnp.zeros(root_ref.shape, BF16)

    def emit(start, base, panel):
        root_ref[start : start + BLOCK, base:] = upper_mask(panel, start, base).astype(BF16)

    factor(work, order, order, emit)


def basis_kernel(basis_ref, high_ref, low_ref, q_ref):
    block = basis_ref[...]
    q_ref[...] = (
        dot_bf16(block, high_ref[...], CONTRACT_LAST)
        + dot_bf16(block, low_ref[...], CONTRACT_LAST)
    ).astype(BF16)


def coupled_kernel(partners_ref, rounded_ref, block_ref, chosen_ref, out_ref):
    left = dot_bf16(rounded_ref[...], block_ref[0]).astype(BF16)
    out_ref[0] = dot_bf16(left, chosen_ref[0], CONTRACT_LAST).astype(BF16)


def whole(shape):
    return pl.BlockSpec(shape, lambda *_: (0,) * len(shape))


VMEM_SPEC = pl.BlockSpec(memory_space=pltpu.VMEM)
BIG = pltpu.CompilerParams(vmem_limit_bytes=48 * 1024 * 1024)


def cost(flops, size):
    return pl.CostEstimate(flops=flops, bytes_accessed=size, transcendentals=0)


def sum_group(value, levels):
    count = lax.axis_size("sub")
    size = 1 << levels
    groups = [list(range(low, low + size)) for low in range(0, count, size)]
    if len(groups) == 1:
        return lax.psum(value, "sub")
    return lax.psum(value, "sub", axis_index_groups=groups)


def shards(leaf_basis, transfers, couplings, partners):
    basis, level_transfers = leaf_basis[0, 0], transfers[0, 0]
    blocks, slots = couplings[0, 0], partners[0, 0]
    leaf, order = basis.shape
    levels = level_transfers.shape[0]
    tile_count = len(upper_tiles(order))
    square = (order, order)
    cube = order * order * order
    gram, tiles = pl.pallas_call(
        gram_kernel,
        out_shape=(
            jax.ShapeDtypeStruct(square, F32),
            jax.ShapeDtypeStruct((tile_count * LANES, LANES), F32),
        ),
        in_specs=[VMEM_SPEC] * 2,
        out_specs=(VMEM_SPEC, VMEM_SPEC),
        compiler_params=BIG,
        cost_estimate=cost(2 * cube * 24, leaf * order * 2),
        name="gram",
    )(basis, level_transfers)
    root_tiles = sum_group(tiles, levels)
    rounded, high, low = pl.pallas_call(
        leaf_kernel,
        out_shape=tuple(jax.ShapeDtypeStruct(square, BF16) for _ in range(3)),
        in_specs=[VMEM_SPEC],
        out_specs=(VMEM_SPEC,) * 3,
        scratch_shapes=[pltpu.VMEM((order, 2 * order), F32)],
        compiler_params=BIG,
        cost_estimate=cost(2 * cube * 100, 4 * order * order),
        name="leaf_factor",
    )(gram)
    gathered = lax.all_gather(rounded, "col", axis=0, tiled=False)
    chunk = leaf // 4
    q_leaf = pl.pallas_call(
        basis_kernel,
        grid=(leaf // chunk,),
        out_shape=jax.ShapeDtypeStruct((leaf, order), BF16),
        in_specs=[pl.BlockSpec((chunk, order), lambda i: (i, 0)), whole(square), whole(square)],
        out_specs=pl.BlockSpec((chunk, order), lambda i: (i, 0)),
        compiler_params=BIG,
        cost_estimate=cost(4 * leaf * order * order, leaf * order * 4),
        name="basis",
    )(basis, high, low)
    slot_count = blocks.shape[0]
    one = (1, order, order)
    coupled = pl.pallas_call(
        coupled_kernel,
        grid_spec=pltpu.PrefetchScalarGridSpec(
            num_scalar_prefetch=1,
            grid=(slot_count,),
            in_specs=[
                pl.BlockSpec(square, lambda k, p: (0, 0)),
                pl.BlockSpec(one, lambda k, p: (k, 0, 0)),
                pl.BlockSpec(one, lambda k, p: (p[k], 0, 0)),
            ],
            out_specs=pl.BlockSpec(one, lambda k, p: (k, 0, 0)),
        ),
        out_shape=jax.ShapeDtypeStruct(blocks.shape, BF16),
        compiler_params=BIG,
        cost_estimate=cost(4 * cube * slot_count, slot_count * order * order * 6),
        name="coupled",
    )(slots, rounded, blocks, gathered)
    root = pl.pallas_call(
        root_kernel,
        out_shape=jax.ShapeDtypeStruct(square, BF16),
        in_specs=[VMEM_SPEC],
        out_specs=VMEM_SPEC,
        scratch_shapes=[pltpu.VMEM(square, F32)],
        compiler_params=BIG,
        cost_estimate=cost(2 * cube * 100, 4 * order * order),
        name="root_factor",
    )(root_tiles)
    return (q_leaf[None, None], root[None, None], coupled[None, None])


def solution(mesh):
    in_specs = (
        P("sub", "col", None, None),
        P("sub", "col", None, None, None),
        P("sub", "col", None, None, None),
        P("sub", "col", None),
    )
    out_specs = (
        P("sub", "col", None, None),
        P("sub", "col", None, None),
        P("sub", "col", None, None, None),
    )
    return jax.shard_map(shards, mesh=mesh, in_specs=in_specs, out_specs=out_specs, check_vma=False)
```

time: 683 us -> 134 us (0.20)
  the two profiles are of different devices: /device:TPU:31 before, /device:TPU:0 now
where the time goes in v1:
time: 134 us; the launch traced here: 133 us
  Pallas kernels  58.6 us (44%)
  waiting for transfers between devices  51.1 us (38%)
  between operations  15.5 us (12%)
  local copies, waits for them, and re-layouts  7.87 us (6%)
    psum x1, waiting for transfers between devices, sum_group(): return lax.psum(value, 'sub')  51.1 us
    pallas_call x1, Pallas kernels, shards(): pl.pallas_call(leaf_kernel, out_shape=tuple((jax.ShapeDtypeStruct(square,...  19.4 us
    pallas_call x1, Pallas kernels, shards(): pl.pallas_call(root_kernel, out_shape=jax.ShapeDtypeStruct(square, BF16),...  18.7 us
    pallas_call x1, Pallas kernels, shards(): pl.pallas_call(gram_kernel, out_shape=(jax.ShapeDtypeStruct(square, F32),...  9.49 us
    unnamed x18, local copies, waits for them, and re-layouts  7.87 us
    pallas_call x1, Pallas kernels, shards(): pl.pallas_call(coupled_kernel, grid_spec=pltpu.PrefetchScalarGridSpec(num...  6.84 us
    pallas_call x1, Pallas kernels, shards(): pl.pallas_call(basis_kernel, grid=(leaf // chunk,), out_shape=jax.ShapeDt...  4.05 us
  transfers between devices with their start and end apart: 2, of which 1 were waited for; matrix products, arithmetic and copies ran while one was open for 0% of the time, Pallas kernels for 32%

profile of v1, /device:TPU:0, one launch (start us, length us, event | category | flops | bytes accessed | tf_op | source)
XLA Modules:
  0.0 133.3 jit_solution(1594793249547962026)
XLA Ops:
  8.0 0.0 all-reduce.2.cloned.1.call-start
  8.0 0.0 copy-start.1
  8.1 1.6 %copy-done.1 = bf16[1,1,2048,512]{3,2,1,0:T(8,128)(2,1)S(1)} copy-done((bf16[1,1,2048,512]{3,2,1,0:T(8,128)(2,1)S(1)}, bf16[1,1,2048,512]{3,2,1,0:T(8,128)(2,1)}, u32[]{:S(2)}) %copy-start.1) | copy-done | bytes 2097176
  9.6 0.0 copy-start.4
  9.6 1.4 %copy-done.4 = bf16[1,1,3,512,512]{4,3,2,1,0:T(8,128)(2,1)S(1)} copy-done((bf16[1,1,3,512,512]{4,3,2,1,0:T(8,128)(2,1)S(1)}, bf16[1,1,3,512,512]{4,3,2,1,0:T(8,128)(2,1)}, u32[]{:S(2)}) %copy-start.4) | copy-done | bytes 1572888
  11.0 9.5 %gram.1 = (f32[512,512]{1,0:T(8,128)S(1)}, f32[1280,128]{1,0:T(8,128)}) custom-call(bf16[2048,512]{1,0:T(8,128)(2,1)S(1)} %bitcast.9, bf16[3,512,512]{2,1,0:T(8,128)(2,1)S(1)} %bitcast.12), custom_call_target="tpu_custom_call" | custom-call | flops 6442450944 | bytes 2097152 | tf_op jit(solution)/shard_map/gram/pallas_call | solution.py:193
  20.5 0.0 copy-start.7
  20.5 1.0 copy-done.7
  21.5 0.0 all-reduce.2.cloned.1.call-update
  21.5 0.2 all-gather.3.cloned.1.call-start
  21.8 0.0 copy-start.8
  21.8 1.2 copy-done.8
  23.0 0.0 copy-start.2
  23.0 19.4 %leaf_factor.1 = (bf16[512,512]{1,0:T(8,128)(2,1)}, bf16[512,512]{1,0:T(8,128)(2,1)S(1)}, bf16[512,512]{1,0:T(8,128)(2,1)S(1)}) custom-call(f32[512,512]{1,0:T(8,128)S(1)} %copy-done.8), custom_call_target="tpu_custom_call" | custom-call | flops 26843545600 | bytes 1048576 | tf_op jit(solution)/shard_map/leaf_factor/pallas_call | solution.py:206
  42.4 0.0 all-gather.3.cloned.1.call-update
  42.4 0.0 copy-done.2
  42.5 4.1 %basis.1 = bf16[2048,512]{1,0:T(8,128)(2,1)} custom-call(bf16[2048,512]{1,0:T(8,128)(2,1)S(1)} %bitcast.10, bf16[512,512]{1,0:T(8,128)(2,1)S(1)} %get-tuple-element.9.high_ref, bf16[512,512]{1,0:T(8,128)(2,1)S(1)} %get-tuple-element.10.low_ref), custom_call_target="tpu_custom_call" | custom-call | flops 2147483648 | bytes 4194304 | tf_op jit(solution)/shard_map/basis/pallas_call | solution.py:218
  46.5 0.0 copy-start
  46.5 51.1 %all-reduce.2.cloned.1.call-done.tiles_ref = f32[1280,128]{1,0:T(8,128)} async-done(((f32[1280,128]{1,0:T(8,128)}), f32[1280,128]{1,0:T(8,128)}) %all-reduce.2.cloned.1.call-update) | async-done | bytes 655376 | tf_op jit(solution)/shard_map/psum | solution.py:181
  97.6 0.0 copy-start.5
  97.6 1.1 copy-done.5
  98.7 0.0 copy-start.6
  98.7 18.7 %root_factor.1 = bf16[512,512]{1,0:T(8,128)(2,1)} custom-call(f32[1280,128]{1,0:T(8,128)S(1)} %copy-done.5), custom_call_target="tpu_custom_call" | custom-call | flops 26843545600 | bytes 1048576 | tf_op jit(solution)/shard_map/root_factor/pallas_call | solution.py:247
  117.4 0.0 all-gather.3.cloned.1.call-done
  117.4 0.0 copy-done
  117.4 0.0 copy-done.6
  117.4 0.0 copy-start.3
  117.4 1.6 %copy-done.3 = bf16[2048,512]{1,0:T(8,128)(2,1)S(1)} copy-done((bf16[2048,512]{1,0:T(8,128)(2,1)S(1)}, bf16[2048,512]{1,0:T(8,128)(2,1)}, u32[]{:S(2)}) %copy-start.3) | copy-done | bytes 2097176
  119.0 6.8 %coupled.1 = bf16[6,512,512]{2,1,0:T(8,128)(2,1)} custom-call(s32[6]{0:T(128)S(1)} %bitcast.13, bf16[512,512]{1,0:T(8,128)(2,1)} %get-tuple-element.12.rounded_ref, bf16[6,512,512]{2,1,0:T(8,128)(2,1)S(1)} %bitcast.8, bf16[4,512,512]{2,1,0:T(8,128)(2,1)S(1)} %bitcast.11), custom_call_target="tpu_custom_call" | custom-call | flops 3221225472 | bytes 9437184 | tf_op jit(solution)/shard_map/coupled/pallas_call | solution.py:230
Async XLA Ops:
  8.0 89.6 %all-reduce.2.cloned.1.call-start = ((), (), s32[]{:S(2)}) async-start(), calls=%async_computation | async-start | bytes 1310720 | tf_op jit(solution)/shard_map/psum | solution.py:181
  8.0 1.6 %copy-start.1 = (bf16[1,1,2048,512]{3,2,1,0:T(8,128)(2,1)S(1)}, bf16[1,1,2048,512]{3,2,1,0:T(8,128)(2,1)}, u32[]{:S(2)}) copy-start(bf16[1,1,2048,512]{3,2,1,0:T(8,128)(2,1)} %param.4) | copy-start | bytes 6291460
  9.6 1.4 %copy-start.4 = (bf16[1,1,3,512,512]{4,3,2,1,0:T(8,128)(2,1)S(1)}, bf16[1,1,3,512,512]{4,3,2,1,0:T(8,128)(2,1)}, u32[]{:S(2)}) copy-start(bf16[1,1,3,512,512]{4,3,2,1,0:T(8,128)(2,1)} %param.5) | copy-start | bytes 4718596
  20.5 1.0 copy-start.7
  21.5 95.9 %all-gather.3.cloned.1.call-start = ((), (), s32[]{:S(2)}) async-start(), calls=%async_computation.1 | async-start | bytes 2621440 | tf_op jit(solution)/shard_map/all_gather | solution.py:216
  21.8 1.2 copy-start.8
  23.0 19.5 %copy-start.2 = (bf16[1,1,2048,512]{3,2,1,0:T(8,128)(2,1)S(1)}, bf16[1,1,2048,512]{3,2,1,0:T(8,128)(2,1)}, u32[]{:S(2)}) copy-start(bf16[1,1,2048,512]{3,2,1,0:T(8,128)(2,1)} %param.4) | copy-start | bytes 6291460
  46.5 70.9 %copy-start = (bf16[1,1,6,512,512]{4,3,2,1,0:T(8,128)(2,1)S(1)}, bf16[1,1,6,512,512]{4,3,2,1,0:T(8,128)(2,1)}, u32[]{:S(2)}) copy-start(bf16[1,1,6,512,512]{4,3,2,1,0:T(8,128)(2,1)} %param.6) | copy-start | bytes 9437188
  97.6 1.1 copy-start.5
  98.7 18.8 %copy-start.6 = (s32[1,1,6]{2,1,0:T(1,128)S(1)}, s32[1,1,6]{2,1,0:T(1,128)}, u32[]{:S(2)}) copy-start(s32[1,1,6]{2,1,0:T(1,128)} %param.7) | copy-start | bytes 76
  117.4 1.6 %copy-start.3 = (bf16[2048,512]{1,0:T(8,128)(2,1)S(1)}, bf16[2048,512]{1,0:T(8,128)(2,1)}, u32[]{:S(2)}) copy-start(bf16[2048,512]{1,0:T(8,128)(2,1)} %all-gather.3.cloned.1.call-done) | copy-start | bytes 6291460
Sparse Core Ops, SparseCore 0:
  21.6 75.8 all-reduce.1
Sparse Core Ops, SparseCore 1:
  42.5 25.1 all-gather.2

commit v2 on v1

v2 whole, which is shorter than its diff:
```python
import functools

import jax
import jax.numpy as jnp
from jax import lax
from jax.experimental import pallas as pl
from jax.experimental.pallas import tpu as pltpu
from jax.sharding import PartitionSpec as P

highest = lax.Precision.HIGHEST
F32 = jnp.float32
BF16 = jnp.bfloat16
LANES = 128
BLOCK = 64
ROWS = 8
SUM_AT = 4
MESH = pl.DeviceIdType.MESH
CONTRACT_FIRST = (((0,), (0,)), ((), ()))
CONTRACT_LAST = (((1,), (1,)), ((), ()))


def dot_f32(a, b, dims=(((1,), (0,)), ((), ()))):
    return lax.dot_general(a, b, dims, precision=highest, preferred_element_type=F32)


def dot_bf16(a, b, dims=(((1,), (0,)), ((), ()))):
    return lax.dot_general(a, b, dims, preferred_element_type=F32)


def upper_tiles(order):
    count = order // LANES
    return [(i, j) for i in range(count) for j in range(i, count)]


def eliminate(block, offset):
    finished = []
    row_index = lax.broadcasted_iota(jnp.int32, (ROWS, LANES), 0)

    def spread(part, first):
        columns = [part[:, first + j : first + j + 1] for j in range(ROWS)]
        return jnp.stack([jnp.broadcast_to(column, part.shape) for column in columns])

    current = block
    for panel in range(BLOCK // ROWS):
        first = offset + panel * ROWS
        top, rest = current[:ROWS], current[ROWS:]
        below = rest.shape[0] > 0
        top_columns = spread(top, first)
        if below:
            rest_columns = spread(rest, first)
        pivots = top_columns[0]
        for j in range(ROWS):
            lead = top_columns[0]
            if j > 0:
                pivots = jnp.where(row_index == j, lead, pivots)
            inverse = 1.0 / lead[j : j + 1]
            factor = jnp.where(row_index > j, lead * inverse, 0.0)
            pivot_row = top[j : j + 1]
            if below:
                rest_factor = rest_columns[0] * inverse
                rest = rest - rest_factor * pivot_row
            if j + 1 < ROWS:
                later = top_columns[1:]
                values = later[:, j : j + 1]
                top_columns = later - factor[None] * values
                if below:
                    rest_columns = rest_columns[1:] - rest_factor[None] * values
                top = top - factor * pivot_row
        finished.append(top * lax.rsqrt(pivots))
        current = rest
    return jnp.concatenate(finished, axis=0)


def factor(work, order, width, emit, between=None):
    extra = width > order
    lane = lax.broadcasted_iota(jnp.int32, (BLOCK, LANES), 1)
    row = lax.broadcasted_iota(jnp.int32, (BLOCK, LANES), 0)
    for start in range(0, order, BLOCK):
        base = start // LANES * LANES
        offset = start - base
        other = BLOCK - offset
        head = work[start : start + BLOCK, base : base + LANES]
        own_half = (lane >= offset) & (lane < offset + BLOCK)
        unit = jnp.where(lane == row + other, 1.0, 0.0).astype(F32)
        solved = eliminate(jnp.where(own_half, head, unit), offset)
        inverse = solved[:, other : other + BLOCK]
        end = order + base + LANES if extra else order
        panel = dot_f32(inverse, work[start : start + BLOCK, base:end])
        emit(start, base, panel)
        if between is not None:
            between(start // BLOCK)
        for low in range(base + offset * 2, order, LANES):
            shift = low - base
            work[low : low + LANES, low:end] -= dot_f32(
                panel[:, shift : shift + LANES], panel[:, shift:], CONTRACT_FIRST
            )


def dot_exact(a, b):
    high = a.astype(BF16)
    left = a - high.astype(F32)
    middle = left.astype(BF16)
    low = (left - middle.astype(F32)).astype(BF16)
    return dot_bf16(high, b) + (dot_bf16(middle, b) + dot_bf16(low, b))


def projected_gram(gram_ref, transfers_ref, tiles_ref, order):
    moved = dot_bf16(transfers_ref[0], transfers_ref[1]) if transfers_ref.shape[0] > 1 else (
        transfers_ref[0].astype(F32)
    )
    for level in range(2, transfers_ref.shape[0]):
        moved = dot_exact(moved, transfers_ref[level])
    applied = dot_f32(gram_ref[...], moved)
    for index, (i, j) in enumerate(upper_tiles(order)):
        tiles_ref[index * LANES : (index + 1) * LANES, :] = dot_f32(
            moved[:, i * LANES : (i + 1) * LANES],
            applied[:, j * LANES : (j + 1) * LANES],
            CONTRACT_FIRST,
        )


def upper_mask(panel, start, base):
    shape = panel.shape
    lane = lax.broadcasted_iota(jnp.int32, shape, 1) + base
    row = lax.broadcasted_iota(jnp.int32, shape, 0) + start
    return jnp.where(lane >= row, panel, 0.0)


def tree_kernel(
    group,
    basis_ref,
    transfers_ref,
    gathered_ref,
    high_ref,
    low_ref,
    root_ref,
    basis,
    level_transfers,
    work,
    tiles,
    arrived,
    total,
    load_sem,
    sum_send,
    sum_recv,
    back_send,
    back_recv,
    col_send,
    col_recv,
):
    order = root_ref.shape[0]
    cols = gathered_ref.shape[0]
    share = arrived.shape[1]
    sub, col = lax.axis_index("sub"), lax.axis_index("col")
    rank = lax.rem(sub, group)
    group_start = sub - rank

    loads = [
        pltpu.make_async_copy(basis_ref, basis, load_sem.at[0]),
        pltpu.make_async_copy(transfers_ref, level_transfers, load_sem.at[1]),
    ]
    for load in loads:
        load.start()

    def sub_peer(step):
        return group_start + lax.rem(rank + step, group)

    def col_peer(step):
        return lax.rem(col + step, cols)

    barrier = pltpu.get_barrier_semaphore()
    for step in range(1, group):
        pl.semaphore_signal(barrier, inc=1, device_id=(sub_peer(step), col), device_id_type=MESH)
    for step in range(1, cols):
        pl.semaphore_signal(barrier, inc=1, device_id=(sub, col_peer(step)), device_id_type=MESH)
    pl.semaphore_wait(barrier, group - 1 + cols - 1)

    row = lax.broadcasted_iota(jnp.int32, (order, order), 0)
    lane = lax.broadcasted_iota(jnp.int32, (order, order), 1)
    loads[0].wait()
    work[:, :order] = dot_bf16(basis[...], basis[...], CONTRACT_FIRST)
    work[:, order:] = jnp.where(row == lane, 1.0, 0.0).astype(F32)
    loads[1].wait()
    used = len(upper_tiles(order)) * LANES
    if tiles.shape[0] > used:
        tiles[used:, :] = jnp.zeros((tiles.shape[0] - used, LANES), F32)
    projected_gram(work.at[:, :order], level_transfers, tiles, order)

    def rows_of(member):
        return pl.ds(pl.multiple_of(member * share, ROWS), share)

    sums = [
        pltpu.make_async_remote_copy(
            src_ref=tiles.at[rows_of(lax.rem(rank + step, group))],
            dst_ref=arrived.at[step - 1],
            send_sem=sum_send.at[step - 1],
            recv_sem=sum_recv.at[step - 1],
            device_id=(sub_peer(step), col),
            device_id_type=MESH,
        )
        for step in range(1, group)
    ]
    for copy in sums:
        copy.start()
    returns = [
        pltpu.make_async_remote_copy(
            src_ref=total.at[rows_of(rank)],
            dst_ref=total.at[rows_of(rank)],
            send_sem=back_send.at[step - 1],
            recv_sem=back_recv.at[step - 1],
            device_id=(sub_peer(step), col),
            device_id_type=MESH,
        )
        for step in range(1, group)
    ]

    def between(index):
        if index == SUM_AT:
            value = tiles[rows_of(rank), :]
            for step in range(1, group):
                sums[step - 1].wait_recv()
                value = value + arrived[step - 1]
            total[rows_of(rank), :] = value
            for copy in returns:
                copy.start()

    own = gathered_ref.at[col]
    own[...] = jnp.zeros((order, order), BF16)
    high_ref[...] = jnp.zeros(high_ref.shape, BF16)
    low_ref[...] = jnp.zeros(low_ref.shape, BF16)

    def emit_leaf(start, base, panel):
        head = upper_mask(panel[:, : order - base], start, base)
        own[start : start + BLOCK, base:] = head.astype(BF16)
        inverse = panel[:, order - base :]
        high = inverse.astype(BF16)
        high_ref[start : start + BLOCK, : base + LANES] = high
        low_ref[start : start + BLOCK, : base + LANES] = (inverse - high.astype(F32)).astype(BF16)

    factor(work, order, 2 * order, emit_leaf, between)

    shown = [
        pltpu.make_async_remote_copy(
            src_ref=gathered_ref.at[col],
            dst_ref=gathered_ref.at[col],
            send_sem=col_send.at[step - 1],
            recv_sem=col_recv.at[step - 1],
            device_id=(sub, col_peer(step)),
            device_id_type=MESH,
        )
        for step in range(1, cols)
    ]
    for copy in returns:
        copy.wait_recv()
    for copy in shown:
        copy.start()

    for index, (i, j) in enumerate(upper_tiles(order)):
        work[i * LANES : (i + 1) * LANES, j * LANES : (j + 1) * LANES] = total[
            index * LANES : (index + 1) * LANES, :
        ]
    root_ref[...] = jnp.zeros(root_ref.shape, BF16)

    def emit_root(start, base, panel):
        root_ref[start : start + BLOCK, base:] = upper_mask(panel, start, base).astype(BF16)

    factor(work, order, order, emit_root)
    for copy in shown:
        copy.wait()
    for copy in sums + returns:
        copy.wait_send()


def basis_kernel(basis_ref, high_ref, low_ref, q_ref):
    block = basis_ref[...]
    q_ref[...] = (
        dot_bf16(block, high_ref[...], CONTRACT_LAST)
        + dot_bf16(block, low_ref[...], CONTRACT_LAST)
    ).astype(BF16)


def coupled_kernel(partners_ref, rounded_ref, block_ref, chosen_ref, out_ref):
    left = dot_bf16(rounded_ref[0], block_ref[0]).astype(BF16)
    out_ref[0] = dot_bf16(left, chosen_ref[0], CONTRACT_LAST).astype(BF16)


def whole(shape):
    return pl.BlockSpec(shape, lambda *_: (0,) * len(shape))


VMEM_SPEC = pl.BlockSpec(memory_space=pltpu.VMEM)
BIG = pltpu.CompilerParams(vmem_limit_bytes=48 * 1024 * 1024)


def cost(flops, size):
    return pl.CostEstimate(flops=flops, bytes_accessed=size, transcendentals=0)


def shards(leaf_basis, transfers, couplings, partners):
    basis, level_transfers = leaf_basis[0, 0], transfers[0, 0]
    blocks, slots = couplings[0, 0], partners[0, 0]
    leaf, order = basis.shape
    levels = level_transfers.shape[0]
    group = min(1 << levels, lax.axis_size("sub"))
    cols = lax.axis_size("col")
    rows = len(upper_tiles(order)) * LANES
    share = -(-rows // (group * ROWS)) * ROWS
    square = (order, order)
    cube = order * order * order
    pair = max(group - 1, 1)
    across = max(cols - 1, 1)
    gathered, high, low, root = pl.pallas_call(
        functools.partial(tree_kernel, group),
        out_shape=(
            jax.ShapeDtypeStruct((cols,) + square, BF16),
            jax.ShapeDtypeStruct(square, BF16),
            jax.ShapeDtypeStruct(square, BF16),
            jax.ShapeDtypeStruct(square, BF16),
        ),
        in_specs=[pl.BlockSpec(memory_space=pl.ANY)] * 2,
        out_specs=(VMEM_SPEC,) * 4,
        scratch_shapes=[
            pltpu.VMEM(basis.shape, BF16),
            pltpu.VMEM(level_transfers.shape, BF16),
            pltpu.VMEM((order, 2 * order), F32),
            pltpu.VMEM((group * share, LANES), F32),
            pltpu.VMEM((pair, share, LANES), F32),
            pltpu.VMEM((group * share, LANES), F32),
            pltpu.SemaphoreType.DMA((2,)),
            pltpu.SemaphoreType.DMA((pair,)),
            pltpu.SemaphoreType.DMA((pair,)),
            pltpu.SemaphoreType.DMA((pair,)),
            pltpu.SemaphoreType.DMA((pair,)),
            pltpu.SemaphoreType.DMA((across,)),
            pltpu.SemaphoreType.DMA((across,)),
        ],
        compiler_params=pltpu.CompilerParams(
            vmem_limit_bytes=56 * 1024 * 1024, collective_id=0, has_side_effects=True
        ),
        cost_estimate=cost(2 * cube * 200, 4 * leaf * order),
        name="tree",
    )(basis, level_transfers)
    own_slot = lax.axis_index("col").astype(jnp.int32)
    places = jnp.concatenate([slots, own_slot[None]])
    chunk = leaf // 4
    q_leaf = pl.pallas_call(
        basis_kernel,
        grid=(leaf // chunk,),
        out_shape=jax.ShapeDtypeStruct((leaf, order), BF16),
        in_specs=[pl.BlockSpec((chunk, order), lambda i: (i, 0)), whole(square), whole(square)],
        out_specs=pl.BlockSpec((chunk, order), lambda i: (i, 0)),
        compiler_params=BIG,
        cost_estimate=cost(4 * leaf * order * order, leaf * order * 4),
        name="basis",
    )(basis, high, low)
    slot_count = blocks.shape[0]
    one = (1, order, order)
    coupled = pl.pallas_call(
        coupled_kernel,
        grid_spec=pltpu.PrefetchScalarGridSpec(
            num_scalar_prefetch=1,
            grid=(slot_count,),
            in_specs=[
                pl.BlockSpec(one, lambda k, p: (p[slot_count], 0, 0)),
                pl.BlockSpec(one, lambda k, p: (k, 0, 0)),
                pl.BlockSpec(one, lambda k, p: (p[k], 0, 0)),
            ],
            out_specs=pl.BlockSpec(one, lambda k, p: (k, 0, 0)),
        ),
        out_shape=jax.ShapeDtypeStruct(blocks.shape, BF16),
        compiler_params=BIG,
        cost_estimate=cost(4 * cube * slot_count, slot_count * order * order * 6),
        name="coupled",
    )(places, gathered, blocks, gathered)
    return (q_leaf[None, None], root[None, None], coupled[None, None])


def solution(mesh):
    in_specs = (
        P("sub", "col", None, None),
        P("sub", "col", None, None, None),
        P("sub", "col", None, None, None),
        P("sub", "col", None),
    )
    out_specs = (
        P("sub", "col", None, None),
        P("sub", "col", None, None),
        P("sub", "col", None, None, None),
    )
    return jax.shard_map(shards, mesh=mesh, in_specs=in_specs, out_specs=out_specs, check_vma=False)
```

time: 134 us -> 80.7 us (0.60)
  the two profiles are of different devices: /device:TPU:0 before, /device:TPU:31 now
where the time goes in v2:
time: 80.7 us; the launch traced here: 79.2 us
  Pallas kernels  74.9 us (93%)
  local copies, waits for them, and re-layouts  2.88 us (4%)
    pallas_call x1, Pallas kernels, shards(): pl.pallas_call(functools.partial(tree_kernel, group), out_shape=(jax.Shap...  65.3 us
    pallas_call x1, Pallas kernels, shards(): pl.pallas_call(coupled_kernel, grid_spec=pltpu.PrefetchScalarGridSpec(num...  5.8 us
    pallas_call x1, Pallas kernels, shards(): pl.pallas_call(basis_kernel, grid=(leaf // chunk,), out_shape=jax.ShapeDt...  3.81 us
    unnamed x13, local copies, waits for them, and re-layouts  2.88 us

profile of v2, /device:TPU:31, one launch (start us, length us, event | category | flops | bytes accessed | tf_op | source)
XLA Modules:
  0.0 79.2 jit_solution(1418646225984921062)
XLA Ops:
  0.6 0.7 pad_add_fusion.partners_ref
  1.4 0.0 copy-start.1
  1.4 65.3 %tree.1 = (bf16[4,512,512]{2,1,0:T(8,128)(2,1)}, bf16[512,512]{1,0:T(8,128)(2,1)}, bf16[512,512]{1,0:T(8,128)(2,1)}, bf16[512,512]{1,0:T(8,128)(2,1)}) custom-call(bf16[2048,512]{1,0:T(8,128)(2,1)} %bitcast.9, bf16[3,512,512]{2,1,0:T(8,128)(2,1)} %bitcast.12), custom_call_target="tpu_custom_call" | custom-call | flops 53687091200 | bytes 4194304 | tf_op jit(solution)/shard_map/tree/pallas_call | solution.py:312
  66.6 0.0 copy-done.1
  66.7 0.0 copy-start.3
  66.7 1.0 %copy-done.3 = bf16[512,512]{1,0:T(8,128)(2,1)S(1)} copy-done((bf16[512,512]{1,0:T(8,128)(2,1)S(1)}, bf16[512,512]{1,0:T(8,128)(2,1)}, u32[]{:S(2)}) %copy-start.3) | copy-done | bytes 524312
  67.7 0.0 copy-start.4
  67.7 1.0 %copy-done.4 = bf16[512,512]{1,0:T(8,128)(2,1)S(1)} copy-done((bf16[512,512]{1,0:T(8,128)(2,1)S(1)}, bf16[512,512]{1,0:T(8,128)(2,1)}, u32[]{:S(2)}) %copy-start.4) | copy-done | bytes 524312
  68.7 0.0 copy-start
  68.7 0.0 copy-start.2
  68.7 3.8 %basis.1 = bf16[2048,512]{1,0:T(8,128)(2,1)} custom-call(bf16[2048,512]{1,0:T(8,128)(2,1)S(1)} %bitcast.10, bf16[512,512]{1,0:T(8,128)(2,1)S(1)} %copy-done.3, bf16[512,512]{1,0:T(8,128)(2,1)S(1)} %copy-done.4), custom_call_target="tpu_custom_call" | custom-call | flops 2147483648 | bytes 4194304 | tf_op jit(solution)/shard_map/basis/pallas_call | solution.py:346
  72.6 0.0 copy-done
  72.6 0.0 copy-done.2
  72.6 0.0 copy-start.5
  72.6 5.8 %coupled.1 = bf16[6,512,512]{2,1,0:T(8,128)(2,1)} custom-call(s32[7]{0:T(128)S(1)} %pad_add_fusion.partners_ref, bf16[4,512,512]{2,1,0:T(8,128)(2,1)S(1)} %copy-done.2, bf16[6,512,512]{2,1,0:T(8,128)(2,1)S(1)} %bitcast.8, bf16[4,512,512]{2,1,0:T(8,128)(2,1)S(1)} %copy-done.2), custom_call_target="tpu_custom_call" | custom-call | flops 3221225472 | bytes 9437184 | tf_op jit(solution)/shard_map/coupled/pallas_call | solution.py:358
  78.4 0.0 copy-done.5
  78.4 0.8 %copy.8 = bf16[1,1,512,512]{3,2,1,0:T(8,128)(2,1)} copy(bf16[1,1,512,512]{3,2,1,0:T(8,128)(2,1)S(1)} %bitcast.11) | data formatting | bytes 1048576
Async XLA Ops:
  1.4 65.3 %copy-start.1 = (bf16[1,1,2048,512]{3,2,1,0:T(8,128)(2,1)S(1)}, bf16[1,1,2048,512]{3,2,1,0:T(8,128)(2,1)}, u32[]{:S(2)}) copy-start(bf16[1,1,2048,512]{3,2,1,0:T(8,128)(2,1)} %param.4) | copy-start | bytes 6291460
  66.7 1.0 %copy-start.3 = (bf16[512,512]{1,0:T(8,128)(2,1)S(1)}, bf16[512,512]{1,0:T(8,128)(2,1)}, u32[]{:S(2)}) copy-start(bf16[512,512]{1,0:T(8,128)(2,1)} %get-tuple-element.7.high_ref) | copy-start | bytes 1572868
  67.7 1.0 %copy-start.4 = (bf16[512,512]{1,0:T(8,128)(2,1)S(1)}, bf16[512,512]{1,0:T(8,128)(2,1)}, u32[]{:S(2)}) copy-start(bf16[512,512]{1,0:T(8,128)(2,1)} %get-tuple-element.8.low_ref) | copy-start | bytes 1572868
  68.7 3.8 %copy-start = (bf16[1,1,6,512,512]{4,3,2,1,0:T(8,128)(2,1)S(1)}, bf16[1,1,6,512,512]{4,3,2,1,0:T(8,128)(2,1)}, u32[]{:S(2)}) copy-start(bf16[1,1,6,512,512]{4,3,2,1,0:T(8,128)(2,1)} %param.6) | copy-start | bytes 9437188
  68.7 3.8 %copy-start.2 = (bf16[4,512,512]{2,1,0:T(8,128)(2,1)S(1)}, bf16[4,512,512]{2,1,0:T(8,128)(2,1)}, u32[]{:S(2)}) copy-start(bf16[4,512,512]{2,1,0:T(8,128)(2,1)} %get-tuple-element.10.rounded_ref.chosen_ref) | copy-start | bytes 6291460
  72.6 5.8 %copy-start.5 = (bf16[512,512]{1,0:T(8,128)(2,1)S(1)}, bf16[512,512]{1,0:T(8,128)(2,1)}, u32[]{:S(2)}) copy-start(bf16[512,512]{1,0:T(8,128)(2,1)} %get-tuple-element.9) | copy-start | bytes 1572868

commit v3 on v2

--- a/solution.py
+++ b/solution.py
@@ -13,7 +13,7 @@
 LANES = 128
 BLOCK = 64
 ROWS = 8
-SUM_AT = 4
+SUM_BEFORE = 2
 MESH = pl.DeviceIdType.MESH
 CONTRACT_FIRST = (((0,), (0,)), ((), ()))
 CONTRACT_LAST = (((1,), (1,)), ((), ()))
@@ -53,8 +53,8 @@
             lead = top_columns[0]
             if j > 0:
                 pivots = jnp.where(row_index == j, lead, pivots)
-            inverse = 1.0 / lead[j : j + 1]
-            factor = jnp.where(row_index > j, lead * inverse, 0.0)
+            inverse = pl.reciprocal(lead[j : j + 1], approx=True)
+            factor = jnp.where(row_index > j, lead, 0.0) * inverse
             pivot_row = top[j : j + 1]
             if below:
                 rest_factor = rest_columns[0] * inverse
@@ -75,17 +75,25 @@
     extra = width > order
     lane = lax.broadcasted_iota(jnp.int32, (BLOCK, LANES), 1)
     row = lax.broadcasted_iota(jnp.int32, (BLOCK, LANES), 0)
+    head = work[:BLOCK, :LANES]
     for start in range(0, order, BLOCK):
         base = start // LANES * LANES
         offset = start - base
         other = BLOCK - offset
-        head = work[start : start + BLOCK, base : base + LANES]
         own_half = (lane >= offset) & (lane < offset + BLOCK)
         unit = jnp.where(lane == row + other, 1.0, 0.0).astype(F32)
         solved = eliminate(jnp.where(own_half, head, unit), offset)
         inverse = solved[:, other : other + BLOCK]
+        following = start + BLOCK
+        if following < order:
+            ahead = following // LANES * LANES
+            near = dot_f32(inverse, work[start:following, ahead : ahead + LANES])
+            shift = following - ahead
+            head = work[following : following + BLOCK, ahead : ahead + LANES] - dot_f32(
+                near[:, shift : shift + BLOCK], near, CONTRACT_FIRST
+            )
         end = order + base + LANES if extra else order
-        panel = dot_f32(inverse, work[start : start + BLOCK, base:end])
+        panel = dot_f32(inverse, work[start:following, base:end])
         emit(start, base, panel)
         if between is not None:
             between(start // BLOCK)
@@ -96,27 +104,38 @@
             )
 
 
-def dot_exact(a, b):
+def parts_of(a):
     high = a.astype(BF16)
     left = a - high.astype(F32)
     middle = left.astype(BF16)
-    low = (left - middle.astype(F32)).astype(BF16)
-    return dot_bf16(high, b) + (dot_bf16(middle, b) + dot_bf16(low, b))
+    return high, middle, (left - middle.astype(F32)).astype(BF16)
 
 
 def projected_gram(gram_ref, transfers_ref, tiles_ref, order):
-    moved = dot_bf16(transfers_ref[0], transfers_ref[1]) if transfers_ref.shape[0] > 1 else (
-        transfers_ref[0].astype(F32)
-    )
-    for level in range(2, transfers_ref.shape[0]):
-        moved = dot_exact(moved, transfers_ref[level])
-    applied = dot_f32(gram_ref[...], moved)
-    for index, (i, j) in enumerate(upper_tiles(order)):
-        tiles_ref[index * LANES : (index + 1) * LANES, :] = dot_f32(
-            moved[:, i * LANES : (i + 1) * LANES],
-            applied[:, j * LANES : (j + 1) * LANES],
-            CONTRACT_FIRST,
+    current = gram_ref[...]
+    levels = transfers_ref.shape[0]
+    for level in range(levels):
+        transfer = transfers_ref[level]
+        high, middle, low = parts_of(current)
+        applied = dot_bf16(high, transfer) + (
+            dot_bf16(middle, transfer) + dot_bf16(low, transfer)
         )
+        high, middle, low = parts_of(applied)
+        if level + 1 < levels:
+            current = dot_bf16(transfer, high, CONTRACT_FIRST) + (
+                dot_bf16(transfer, middle, CONTRACT_FIRST)
+                + dot_bf16(transfer, low, CONTRACT_FIRST)
+            )
+    start = 0
+    for first in range(0, order, LANES):
+        left = transfers_ref[levels - 1, :, first : first + LANES]
+        strip = dot_bf16(left, high[:, first:], CONTRACT_FIRST) + (
+            dot_bf16(left, middle[:, first:], CONTRACT_FIRST)
+            + dot_bf16(left, low[:, first:], CONTRACT_FIRST)
+        )
+        for column in range(0, order - first, LANES):
+            tiles_ref[start : start + LANES, :] = strip[:, column : column + LANES]
+            start += LANES
 
 
 def upper_mask(panel, start, base):
@@ -130,12 +149,16 @@
     group,
     basis_ref,
     transfers_ref,
+    blocks_ref,
     gathered_ref,
-    high_ref,
-    low_ref,
+    q_ref,
+    left_ref,
     root_ref,
     basis,
     level_transfers,
+    blocks,
+    high_ref,
+    low_ref,
     work,
     tiles,
     arrived,
@@ -158,6 +181,7 @@
     loads = [
         pltpu.make_async_copy(basis_ref, basis, load_sem.at[0]),
         pltpu.make_async_copy(transfers_ref, level_transfers, load_sem.at[1]),
+        pltpu.make_async_copy(blocks_ref, blocks, load_sem.at[2]),
     ]
     for load in loads:
         load.start()
@@ -214,8 +238,26 @@
         for step in range(1, group)
     ]
 
+    half = order // 2
+    shown = [
+        pltpu.make_async_remote_copy(
+            src_ref=gathered_ref.at[col, pl.ds(part * half, half)],
+            dst_ref=gathered_ref.at[col, pl.ds(part * half, half)],
+            send_sem=col_send.at[part, step - 1],
+            recv_sem=col_recv.at[part, step - 1],
+            device_id=(sub, col_peer(step)),
+            device_id_type=MESH,
+        )
+        for part in range(2)
+        for step in range(1, cols)
+    ]
+    early, late = shown[: cols - 1], shown[cols - 1 :]
+
     def between(index):
-        if index == SUM_AT:
+        if (index + 1) * BLOCK == half:
+            for copy in early:
+                copy.start()
+        if (index + 1) * BLOCK == order - SUM_BEFORE * BLOCK:
             value = tiles[rows_of(rank), :]
             for step in range(1, group):
                 sums[step - 1].wait_recv()
@@ -239,21 +281,21 @@
 
     factor(work, order, 2 * order, emit_leaf, between)
 
-    shown = [
-        pltpu.make_async_remote_copy(
-            src_ref=gathered_ref.at[col],
-            dst_ref=gathered_ref.at[col],
-            send_sem=col_send.at[step - 1],
-            recv_sem=col_recv.at[step - 1],
-            device_id=(sub, col_peer(step)),
-            device_id_type=MESH,
-        )
-        for step in range(1, cols)
-    ]
+    for copy in late:
+        copy.start()
+    chunk = order
+    for low in range(0, basis.shape[0], chunk):
+        rows = basis[low : low + chunk, :]
+        q_ref[low : low + chunk, :] = (
+            dot_bf16(rows, high_ref[...], CONTRACT_LAST)
+            + dot_bf16(rows, low_ref[...], CONTRACT_LAST)
+        ).astype(BF16)
+    loads[2].wait()
+    rounded = own[...]
+    for slot in range(blocks.shape[0]):
+        left_ref[slot] = dot_bf16(rounded, blocks[slot]).astype(BF16)
     for copy in returns:
         copy.wait_recv()
-    for copy in shown:
-        copy.start()
 
     for index, (i, j) in enumerate(upper_tiles(order)):
         work[i * LANES : (i + 1) * LANES, j * LANES : (j + 1) * LANES] = total[
@@ -271,21 +313,8 @@
         copy.wait_send()
 
 
-def basis_kernel(basis_ref, high_ref, low_ref, q_ref):
-    block = basis_ref[...]
-    q_ref[...] = (
-        dot_bf16(block, high_ref[...], CONTRACT_LAST)
-        + dot_bf16(block, low_ref[...], CONTRACT_LAST)
-    ).astype(BF16)
-
-
-def coupled_kernel(partners_ref, rounded_ref, block_ref, chosen_ref, out_ref):
-    left = dot_bf16(rounded_ref[0], block_ref[0]).astype(BF16)
-    out_ref[0] = dot_bf16(left, chosen_ref[0], CONTRACT_LAST).astype(BF16)
-
-
-def whole(shape):
-    return pl.BlockSpec(shape, lambda *_: (0,) * len(shape))
+def coupled_kernel(partners_ref, left_ref, chosen_ref, out_ref):
+    out_ref[0] = dot_bf16(left_ref[0], chosen_ref[0], CONTRACT_LAST).astype(BF16)
 
 
 VMEM_SPEC = pl.BlockSpec(memory_space=pltpu.VMEM)
@@ -309,50 +338,40 @@
     cube = order * order * order
     pair = max(group - 1, 1)
     across = max(cols - 1, 1)
-    gathered, high, low, root = pl.pallas_call(
+    gathered, q_leaf, left, root = pl.pallas_call(
         functools.partial(tree_kernel, group),
         out_shape=(
             jax.ShapeDtypeStruct((cols,) + square, BF16),
-            jax.ShapeDtypeStruct(square, BF16),
-            jax.ShapeDtypeStruct(square, BF16),
+            jax.ShapeDtypeStruct(basis.shape, BF16),
+            jax.ShapeDtypeStruct(blocks.shape, BF16),
             jax.ShapeDtypeStruct(square, BF16),
         ),
-        in_specs=[pl.BlockSpec(memory_space=pl.ANY)] * 2,
+        in_specs=[pl.BlockSpec(memory_space=pl.ANY)] * 3,
         out_specs=(VMEM_SPEC,) * 4,
         scratch_shapes=[
             pltpu.VMEM(basis.shape, BF16),
             pltpu.VMEM(level_transfers.shape, BF16),
+            pltpu.VMEM(blocks.shape, BF16),
+            pltpu.VMEM(square, BF16),
+            pltpu.VMEM(square, BF16),
             pltpu.VMEM((order, 2 * order), F32),
             pltpu.VMEM((group * share, LANES), F32),
             pltpu.VMEM((pair, share, LANES), F32),
             pltpu.VMEM((group * share, LANES), F32),
-            pltpu.SemaphoreType.DMA((2,)),
+            pltpu.SemaphoreType.DMA((3,)),
             pltpu.SemaphoreType.DMA((pair,)),
             pltpu.SemaphoreType.DMA((pair,)),
             pltpu.SemaphoreType.DMA((pair,)),
             pltpu.SemaphoreType.DMA((pair,)),
-            pltpu.SemaphoreType.DMA((across,)),
-            pltpu.SemaphoreType.DMA((across,)),
+            pltpu.SemaphoreType.DMA((2, across)),
+            pltpu.SemaphoreType.DMA((2, across)),
         ],
         compiler_params=pltpu.CompilerParams(
             vmem_limit_bytes=56 * 1024 * 1024, collective_id=0, has_side_effects=True
         ),
         cost_estimate=cost(2 * cube * 200, 4 * leaf * order),
         name="tree",
-    )(basis, level_transfers)
-    own_slot = lax.axis_index("col").astype(jnp.int32)
-    places = jnp.concatenate([slots, own_slot[None]])
-    chunk = leaf // 4
-    q_leaf = pl.pallas_call(
-        basis_kernel,
-        grid=(leaf // chunk,),
-        out_shape=jax.ShapeDtypeStruct((leaf, order), BF16),
-        in_specs=[pl.BlockSpec((chunk, order), lambda i: (i, 0)), whole(square), whole(square)],
-        out_specs=pl.BlockSpec((chunk, order), lambda i: (i, 0)),
-        compiler_params=BIG,
-        cost_estimate=cost(4 * leaf * order * order, leaf * order * 4),
-        name="basis",
-    )(basis, high, low)
+    )(basis, level_transfers, blocks)
     slot_count = blocks.shape[0]
     one = (1, order, order)
     coupled = pl.pallas_call(
@@ -361,7 +380,6 @@
             num_scalar_prefetch=1,
             grid=(slot_count,),
             in_specs=[
-                pl.BlockSpec(one, lambda k, p: (p[slot_count], 0, 0)),
                 pl.BlockSpec(one, lambda k, p: (k, 0, 0)),
                 pl.BlockSpec(one, lambda k, p: (p[k], 0, 0)),
             ],
@@ -371,7 +389,7 @@
         compiler_params=BIG,
         cost_estimate=cost(4 * cube * slot_count, slot_count * order * order * 6),
         name="coupled",
-    )(places, gathered, blocks, gathered)
+    )(slots, left, gathered)
     return (q_leaf[None, None], root[None, None], coupled[None, None])
 
 

time: 80.7 us -> 73.9 us (0.916); the launches traced: 79.2 us -> 73.7 us
  Pallas kernels: 74.9 us -> 67.3 us
  local copies, waits for them, and re-layouts: 2.88 us -> 5.67 us
    pallas_call x1 -> x0, Pallas kernels: 3.81 us -> none  [shards(): pl.pallas_call(basis_kernel, grid=(leaf // chunk,), out_shape=jax.ShapeDt...]
    unnamed x13 -> x12, local copies, waits for them, and re-layouts: 2.88 us -> 5.67 us
    pallas_call x1, Pallas kernels: 65.3 us -> 62.5 us  [shards(): pl.pallas_call(functools.partial(tree_kernel, group), out_shape=(jax.Shap...]
    pallas_call x1, Pallas kernels: 5.8 us -> 4.84 us  [shards(): pl.pallas_call(coupled_kernel, grid_spec=pltpu.PrefetchScalarGridSpec(num...]
where the time goes in v3:
time: 73.9 us; the launch traced here: 73.7 us
  Pallas kernels  67.3 us (91%)
  local copies, waits for them, and re-layouts  5.67 us (8%)
    pallas_call x1, Pallas kernels, shards(): pl.pallas_call(functools.partial(tree_kernel, group), out_shape=(jax.Shap...  62.5 us
    unnamed x12, local copies, waits for them, and re-layouts  5.67 us
    pallas_call x1, Pallas kernels, shards(): pl.pallas_call(coupled_kernel, grid_spec=pltpu.PrefetchScalarGridSpec(num...  4.84 us

profile of v3, /device:TPU:31, one launch (start us, length us, event | category | flops | bytes accessed | tf_op | source)
XLA Modules:
  0.0 73.7 jit_solution(15297098707699762844)
XLA Ops:
  0.6 0.0 copy-start
  0.6 62.5 %tree.1 = (bf16[4,512,512]{2,1,0:T(8,128)(2,1)}, bf16[2048,512]{1,0:T(8,128)(2,1)}, bf16[6,512,512]{2,1,0:T(8,128)(2,1)}, bf16[512,512]{1,0:T(8,128)(2,1)}) custom-call(bf16[2048,512]{1,0:T(8,128)(2,1)} %bitcast.11, bf16[3,512,512]{2,1,0:T(8,128)(2,1)} %bitcast.12, bf16[6,512,512]{2,1,0:T(8,128)(2,1)} %bitcast.10), custom_call_target="tpu_custom_call" | custom-call | flops 53687091200 | bytes 4194304 | tf_op jit(solution)/shard_map/tree/pallas_call | solution.py:341
  63.2 0.0 copy-done
  63.2 0.0 copy-start.1
  63.2 1.9 %copy-done.1 = bf16[6,512,512]{2,1,0:T(8,128)(2,1)S(1)} copy-done((bf16[6,512,512]{2,1,0:T(8,128)(2,1)S(1)}, bf16[6,512,512]{2,1,0:T(8,128)(2,1)}, u32[]{:S(2)}) %copy-start.1) | copy-done | bytes 3145752
  65.1 0.0 copy-start.2
  65.1 1.6 %copy-done.2 = bf16[4,512,512]{2,1,0:T(8,128)(2,1)S(1)} copy-done((bf16[4,512,512]{2,1,0:T(8,128)(2,1)S(1)}, bf16[4,512,512]{2,1,0:T(8,128)(2,1)}, u32[]{:S(2)}) %copy-start.2) | copy-done | bytes 2097176
  66.6 0.0 copy-start.3
  66.6 4.8 %coupled.1 = bf16[6,512,512]{2,1,0:T(8,128)(2,1)} custom-call(s32[6]{0:T(128)S(1)} %bitcast.7, bf16[6,512,512]{2,1,0:T(8,128)(2,1)S(1)} %copy-done.1, bf16[4,512,512]{2,1,0:T(8,128)(2,1)S(1)} %copy-done.2), custom_call_target="tpu_custom_call" | custom-call | flops 3221225472 | bytes 9437184 | tf_op jit(solution)/shard_map/coupled/pallas_call | solution.py:377
  71.5 0.0 copy-done.3
  71.5 0.0 copy-start.4
  71.5 1.3 %copy.9 = bf16[1,1,2048,512]{3,2,1,0:T(8,128)(2,1)} copy(bf16[1,1,2048,512]{3,2,1,0:T(8,128)(2,1)S(1)} %bitcast.8) | data formatting | bytes 4194304
  72.8 0.1 copy-done.4
  72.9 0.8 %copy.10 = bf16[1,1,512,512]{3,2,1,0:T(8,128)(2,1)} copy(bf16[1,1,512,512]{3,2,1,0:T(8,128)(2,1)S(1)} %bitcast.9) | data formatting | bytes 1048576
Async XLA Ops:
  0.6 62.5 %copy-start = (s32[1,1,6]{2,1,0:T(1,128)S(1)}, s32[1,1,6]{2,1,0:T(1,128)}, u32[]{:S(2)}) copy-start(s32[1,1,6]{2,1,0:T(1,128)} %param.7) | copy-start | bytes 76
  63.2 1.9 %copy-start.1 = (bf16[6,512,512]{2,1,0:T(8,128)(2,1)S(1)}, bf16[6,512,512]{2,1,0:T(8,128)(2,1)}, u32[]{:S(2)}) copy-start(bf16[6,512,512]{2,1,0:T(8,128)(2,1)} %get-tuple-element.9.left_ref) | copy-start | bytes 9437188
  65.1 1.6 %copy-start.2 = (bf16[4,512,512]{2,1,0:T(8,128)(2,1)S(1)}, bf16[4,512,512]{2,1,0:T(8,128)(2,1)}, u32[]{:S(2)}) copy-start(bf16[4,512,512]{2,1,0:T(8,128)(2,1)} %get-tuple-element.10.chosen_ref) | copy-start | bytes 6291460
  66.6 4.8 %copy-start.3 = (bf16[2048,512]{1,0:T(8,128)(2,1)S(1)}, bf16[2048,512]{1,0:T(8,128)(2,1)}, u32[]{:S(2)}) copy-start(bf16[2048,512]{1,0:T(8,128)(2,1)} %get-tuple-element.7) | copy-start | bytes 6291460
  71.5 1.4 %copy-start.4 = (bf16[512,512]{1,0:T(8,128)(2,1)S(1)}, bf16[512,512]{1,0:T(8,128)(2,1)}, u32[]{:S(2)}) copy-start(bf16[512,512]{1,0:T(8,128)(2,1)} %get-tuple-element.8) | copy-start | bytes 1572868
